TPU v7x, 32 devices: a whole 2x2x4 slice. The times are simulated.
32 devices in a mesh: cells: 8 (over z, core), tracer: 4 (over y, x).
Axes of the slice: x: 2, y: 2, z: 4, core: 2. Of those that a mesh axis runs over, the one named last changes fastest.
Arguments:
- adjoint: float32 [64, 32768], P('tracer', 'cells'), may hold values from -6 to 6
- blocks: float32 [1024, 128, 128], P('cells'), may hold values from -0.375 to 0.375
- row_ptr: int32 [8, 33], P('cells'), may hold values from 0 to 128, as said below
- col_idx: int32 [1024], P('cells'), may hold values from 0 to 255, as said below
- regime: int32 [256], P('cells'), may hold values from 0 to 7
- jac: float32 [8, 64, 64], replicated, as said below
Outputs:
- sensitivity: float32 [64, 32768], P('tracer', 'cells')
Inputs may be any that keep to these rules, and one draw needn't show every extreme that they name: row_ptr[d, 0] = 0 and each block row holds 1 to 4 slots; some index of cells uses all 128 slots. `col_idx`: the first slot of each block row is its diagonal block; a live slot's column lies at most 32 blocks away from its block row, counted cyclically over the 256 blocks, and that distance is reached; slots past row_ptr[d, 32] hold any valid column. `jac`: each regime's matrix has diagonal entries of order one and off-diagonal couplings of order 0.1 between every pair of species.
All inputs are finite; a program needn't handle non-finite values.
Results may differ from a plain program's by a relative error of at most 0.0001.
Values sent between devices are 32-bit elements; how exact they have to be, the bound alone decides.
A program may use at most 64 MiB of HBM per device.

v0:
```python
import jax
import jax.numpy as jnp
from jax import lax
from jax.sharding import PartitionSpec as P

BLOCK = 128
STEPS = 2


def with_halo(cells, sides, width):
    for axis, dim in sides:
        count = lax.axis_size(axis)
        head = lax.slice_in_dim(cells, 0, width, axis=dim)
        tail = lax.slice_in_dim(cells, cells.shape[dim] - width, cells.shape[dim], axis=dim)
        cells = jnp.concatenate(
            [
                lax.ppermute(tail, axis, [(i, (i + 1) % count) for i in range(count)]),
                cells,
                lax.ppermute(head, axis, [((i + 1) % count, i) for i in range(count)]),
            ],
            axis=dim,
        )
    return cells


def chemistry(moved, cell_regime, jac_table):
    result = jnp.zeros((jac_table.shape[2], moved.shape[1]), jnp.float32)
    for regime_id in range(jac_table.shape[0]):
        reacted = jnp.einsum(
            "ts,tc->sc", jac_table[regime_id], moved, precision=lax.Precision.HIGHEST
        )
        result = result + jnp.where(
            cell_regime[None, :] == regime_id, reacted, jnp.zeros_like(reacted)
        )
    return result


def body(adjoint, blocks, row_ptr, col_idx, regime, jac):
    spec_dev, cells_dev = adjoint.shape
    nb_dev = cells_dev // BLOCK
    cell_devices = lax.axis_size("cells")
    cell_index = lax.axis_index("cells")
    tracer_index = lax.axis_index("tracer")
    nb_total = nb_dev * cell_devices
    pointers = row_ptr[0]
    slot_count = blocks.shape[0]
    slot_ids = jnp.arange(slot_count)
    member = (
        (slot_ids[None, :] >= pointers[:-1, None]) & (slot_ids[None, :] < pointers[1:, None])
    ).astype(jnp.float32)
    live_slot = slot_ids < pointers[-1]
    local_col = jnp.mod(col_idx - (cell_index - 1) * nb_dev, nb_total)
    local_col = jnp.where(live_slot, local_col, 0)
    cell_regime = jnp.repeat(regime, BLOCK)
    adjoint_field = adjoint
    for hour_step in range(STEPS):
        extended = with_halo(adjoint_field, (("cells", 1),), cells_dev)
        extended_blocks = extended.reshape(spec_dev, 3 * nb_dev, BLOCK)
        picked = jnp.take(extended_blocks, local_col, axis=1, mode="clip")
        picked = jnp.where(live_slot[None, :, None], picked, jnp.zeros_like(picked))
        products = jnp.einsum("sij,qsj->qsi", blocks, picked, precision=lax.Precision.HIGHEST)
        moved = jnp.einsum(
            "rs,qsi->qri", member, products, precision=lax.Precision.HIGHEST
        ).reshape(spec_dev, cells_dev)
        whole = lax.all_gather(moved, "tracer", axis=0, tiled=True)
        species_rows = lax.dynamic_slice_in_dim(jac, tracer_index * spec_dev, spec_dev, 2)
        adjoint_field = chemistry(whole, cell_regime, species_rows)
    return adjoint_field


def solution(mesh):
    return jax.shard_map(
        body,
        mesh=mesh,
        in_specs=(
            P("tracer", "cells"),
            P("cells", None, None),
            P("cells", None),
            P("cells"),
            P("cells"),
            P(),
        ),
        out_specs=P("tracer", "cells"),
        check_vma=False,
    )
```

profile of v0, /device:TPU:0, one launch (start us, length us, event | category | flops | bytes accessed | tf_op | source)
XLA Modules:
  0.0 147.5 jit_solution(12921534344119128744)
XLA Ops:
  6.5 0.0 copy-start
  6.5 0.0 copy-start.3
  6.5 0.0 all-gather.3.cloned.1.call-start
  6.5 0.5 collective-permute-start
  7.0 4.1 %collective-permute-start.1 = (f32[16,4096]{1,0:T(8,128)}, f32[16,4096]{1,0:T(8,128)S(1)}, u32[]{:S(2)}, u32[]{:S(2)}) collective-permute-start(f32[16,4096]{1,0:T(8,128)} %param.6), channel_id=1, source_target_pairs={{4,0},{8,4},{12,8},{16,12},{20,16},{24,20},{28,24},{0,28},{5,1},{9... | collective-permute-start | bytes 786440 | tf_op jit(solution)/shard_map/ppermute | solution.py:19
  11.1 1.2 slice.45
  12.3 1.3 fusion.50
  13.6 0.7 iota_compare_fusion.2
  14.3 0.8 slice_bitcast_fusion.1
  15.1 0.4 collective-permute-done
  15.5 0.6 collective-permute-done.1
  16.1 1.0 copy_bitcast_fusion.1
  17.1 0.8 gather_fusion
  17.8 15.5 %convolution_bitcast_fusion.1 = f32[16,128,128]{2,0,1:T(8,128)S(1)} fusion(f32[128,128,128]{2,1,0:T(8,128)} %param.7, f32[128,16,128]{2,1,0:T(8,128)S(1)} %gather_fusion, pred[128]{0:T(512)(128)(4,1)S(1)} %iota_compare_fusion.2), kind=kOutput, calls=%fused_computation.33 | convolution fusion | flops 402915328 | bytes 10485888 | tf_op jit(solution)/shard_map/sij,qsj->qsi/dot_general | solution.py:61
  33.3 0.7 fusion.18
  34.1 0.9 copy.25
  34.9 0.0 all-gather.3.cloned.1.call-update
  34.9 0.2 all-gather.5.cloned.1.call-start
  35.2 0.0 copy-done.3
  35.2 0.1 broadcast_bitcast_fusion.6
  35.3 0.1 broadcast_bitcast_fusion.4
  35.4 0.1 broadcast_bitcast_fusion.2
  35.4 0.1 broadcast_bitcast_fusion
  35.5 28.2 %all-gather.3.cloned.1.call-done = f32[64,4096]{1,0:T(8,128)} async-done(((f32[16,4096]{1,0:T(8,128)}), f32[64,4096]{1,0:T(8,128)}) %all-gather.3.cloned.1.call-update) | async-done | bytes 1048592 | tf_op jit(solution)/shard_map/all_gather | solution.py:65
  63.7 0.0 copy-start.1
  63.7 0.0 copy-done
  63.7 2.0 %convolution_select_fusion.15 = f32[16,4096]{1,0:T(8,128)S(1)} fusion(f32[64,4096]{1,0:T(8,128)} %all-gather.3.cloned.1.call-done, pred[4096]{0:T(1024)(128)(4,1)S(1)} %get-tuple-element.22, f32[8,64,64]{2,1,0:T(8,128)S(1)} %copy-done, s32[]{:T(128)S(6)} %select_n.71), kind=kOutput, calls=%fused_computation.31 | convolution fusion | flops 50397184 | bytes 1347588 | tf_op jit(solution)/shard_map/ts,tc->sc/dot_general | solution.py:29
  65.7 1.9 %fusion.13 = f32[16,4096]{1,0:T(8,128)S(1)} fusion(f32[16,4096]{1,0:T(8,128)S(1)} %convolution_select_fusion.15, f32[64,4096]{1,0:T(8,128)} %all-gather.3.cloned.1.call-done, pred[4096]{0:T(1024)(128)(4,1)S(1)} %get-tuple-element.21, f32[8,64,64]{2,1,0:T(8,128)S(1)} %copy-done, s32[]{:T(128)S(6)} %add.69, s32[]{:T(128)S(6)} %select_n.71), kind=kOutput, calls=%fused_computation.30 | convolution fusion | flops 50462720 | bytes 1609736 | tf_op jit(solution)/shard_map/ts,tc->sc/dot_general | solution.py:29
  67.6 1.9 %fusion.12 = f32[16,4096]{1,0:T(8,128)S(1)} fusion(f32[16,4096]{1,0:T(8,128)S(1)} %fusion.13, f32[64,4096]{1,0:T(8,128)} %all-gather.3.cloned.1.call-done, pred[4096]{0:T(1024)(128)(4,1)S(1)} %get-tuple-element.20, f32[8,64,64]{2,1,0:T(8,128)S(1)} %copy-done, s32[]{:T(128)S(6)} %add.70, s32[]{:T(128)S(6)} %select_n.71), kind=kOutput, calls=%fused_computation.28 | convolution fusion | flops 50462720 | bytes 1609736 | tf_op jit(solution)/shard_map/ts,tc->sc/dot_general | solution.py:29
  69.5 1.9 %fusion.11 = f32[16,4096]{1,0:T(8,128)S(1)} fusion(f32[16,4096]{1,0:T(8,128)S(1)} %fusion.12, f32[64,4096]{1,0:T(8,128)} %all-gather.3.cloned.1.call-done, pred[4096]{0:T(1024)(128)(4,1)S(1)} %get-tuple-element.19, f32[8,64,64]{2,1,0:T(8,128)S(1)} %copy-done, s32[]{:T(128)S(6)} %add.71, s32[]{:T(128)S(6)} %select_n.71), kind=kOutput, calls=%fused_computation.26 | convolution fusion | flops 50462720 | bytes 1609736 | tf_op jit(solution)/shard_map/ts,tc->sc/dot_general | solution.py:29
  71.5 1.9 %fusion.10 = f32[16,4096]{1,0:T(8,128)S(1)} fusion(f32[16,4096]{1,0:T(8,128)S(1)} %fusion.11, f32[64,4096]{1,0:T(8,128)} %all-gather.3.cloned.1.call-done, pred[4096]{0:T(1024)(128)(4,1)S(1)} %get-tuple-element.18, f32[8,64,64]{2,1,0:T(8,128)S(1)} %copy-done, s32[]{:T(128)S(6)} %add.72, s32[]{:T(128)S(6)} %select_n.71), kind=kOutput, calls=%fused_computation.24 | convolution fusion | flops 50462720 | bytes 1609736 | tf_op jit(solution)/shard_map/ts,tc->sc/dot_general | solution.py:29
  73.4 0.0 copy-done.1
  73.4 0.7 fusion.9
  74.1 0.7 fusion.8
  74.7 0.7 fusion.7
  75.4 0.1 collective-permute-start.2
  75.5 3.5 %collective-permute-start.3 = (f32[16,4096]{1,0:T(8,128)S(1)}, f32[16,4096]{1,0:T(8,128)S(1)}, u32[]{:S(2)}, u32[]{:S(2)}) collective-permute-start(f32[16,4096]{1,0:T(8,128)S(1)} %fusion.7), channel_id=1, source_target_pairs={{4,0},{8,4},{12,8},{16,12},{20,16},{24,20},{28,24},{0,28},{5,1},{9... | collective-permute-start | bytes 786440 | tf_op jit(solution)/shard_map/ppermute | solution.py:19
  79.0 5.0 %collective-permute-done.2 = f32[16,4096]{1,0:T(8,128)S(1)} collective-permute-done((f32[16,4096]{1,0:T(8,128)S(1)}, f32[16,4096]{1,0:T(8,128)S(1)}, u32[]{:S(2)}, u32[]{:S(2)}) %collective-permute-start.2) | collective-permute-done | bytes 262176 | tf_op jit(solution)/shard_map/ppermute | solution.py:17
  84.0 0.0 collective-permute-done.3
  84.0 0.1 copy_bitcast_fusion
  84.1 0.8 gather_fusion.1
  84.8 15.5 %convolution_bitcast_fusion = f32[16,128,128]{2,0,1:T(8,128)S(1)} fusion(f32[128,128,128]{2,1,0:T(8,128)} %param.7, f32[128,16,128]{2,1,0:T(8,128)S(1)} %gather_fusion.1, pred[128]{0:T(512)(128)(4,1)S(1)} %iota_compare_fusion.2), kind=kOutput, calls=%fused_computation.32 | convolution fusion | flops 402915328 | bytes 10485888 | tf_op jit(solution)/shard_map/sij,qsj->qsi/dot_general | solution.py:61
  100.3 0.7 fusion.16
  101.0 0.9 copy.24
  101.9 0.0 all-gather.5.cloned.1.call-update
  101.9 26.3 %all-gather.5.cloned.1.call-done = f32[64,4096]{1,0:T(8,128)} async-done(((f32[16,4096]{1,0:T(8,128)}), f32[64,4096]{1,0:T(8,128)}) %all-gather.5.cloned.1.call-update) | async-done | bytes 1048592 | tf_op jit(solution)/shard_map/all_gather | solution.py:65
  128.3 0.0 copy-start.2
  128.3 2.0 %convolution_select_fusion.7 = f32[16,4096]{1,0:T(8,128)S(1)} fusion(f32[64,4096]{1,0:T(8,128)} %all-gather.5.cloned.1.call-done, pred[4096]{0:T(1024)(128)(4,1)S(1)} %get-tuple-element.22, f32[8,64,64]{2,1,0:T(8,128)S(1)} %copy-done, s32[]{:T(128)S(6)} %select_n.71), kind=kOutput, calls=%fused_computation.16 | convolution fusion | flops 50397184 | bytes 1347588 | tf_op jit(solution)/shard_map/ts,tc->sc/dot_general | solution.py:29
  130.3 1.9 %fusion.6 = f32[16,4096]{1,0:T(8,128)S(1)} fusion(f32[16,4096]{1,0:T(8,128)S(1)} %convolution_select_fusion.7, f32[64,4096]{1,0:T(8,128)} %all-gather.5.cloned.1.call-done, pred[4096]{0:T(1024)(128)(4,1)S(1)} %get-tuple-element.21, f32[8,64,64]{2,1,0:T(8,128)S(1)} %copy-done, s32[]{:T(128)S(6)} %add.69, s32[]{:T(128)S(6)} %select_n.71), kind=kOutput, calls=%fused_computation.15 | convolution fusion | flops 50462720 | bytes 1609736 | tf_op jit(solution)/shard_map/ts,tc->sc/dot_general | solution.py:29
  132.2 1.9 %fusion.5 = f32[16,4096]{1,0:T(8,128)S(1)} fusion(f32[16,4096]{1,0:T(8,128)S(1)} %fusion.6, f32[64,4096]{1,0:T(8,128)} %all-gather.5.cloned.1.call-done, pred[4096]{0:T(1024)(128)(4,1)S(1)} %get-tuple-element.20, f32[8,64,64]{2,1,0:T(8,128)S(1)} %copy-done, s32[]{:T(128)S(6)} %add.70, s32[]{:T(128)S(6)} %select_n.71), kind=kOutput, calls=%fused_computation.13 | convolution fusion | flops 50462720 | bytes 1609736 | tf_op jit(solution)/shard_map/ts,tc->sc/dot_general | solution.py:29
  134.1 1.9 %fusion.4 = f32[16,4096]{1,0:T(8,128)S(1)} fusion(f32[16,4096]{1,0:T(8,128)S(1)} %fusion.5, f32[64,4096]{1,0:T(8,128)} %all-gather.5.cloned.1.call-done, pred[4096]{0:T(1024)(128)(4,1)S(1)} %get-tuple-element.19, f32[8,64,64]{2,1,0:T(8,128)S(1)} %copy-done, s32[]{:T(128)S(6)} %add.71, s32[]{:T(128)S(6)} %select_n.71), kind=kOutput, calls=%fused_computation.11 | convolution fusion | flops 50462720 | bytes 1609736 | tf_op jit(solution)/shard_map/ts,tc->sc/dot_general | solution.py:29
  136.0 1.9 %fusion.3 = f32[16,4096]{1,0:T(8,128)S(1)} fusion(f32[16,4096]{1,0:T(8,128)S(1)} %fusion.4, f32[64,4096]{1,0:T(8,128)} %all-gather.5.cloned.1.call-done, pred[4096]{0:T(1024)(128)(4,1)S(1)} %get-tuple-element.18, f32[8,64,64]{2,1,0:T(8,128)S(1)} %copy-done, s32[]{:T(128)S(6)} %add.72, s32[]{:T(128)S(6)} %select_n.71), kind=kOutput, calls=%fused_computation.9 | convolution fusion | flops 50462720 | bytes 1609736 | tf_op jit(solution)/shard_map/ts,tc->sc/dot_general | solution.py:29
  137.9 0.0 copy-done.2
  137.9 0.7 fusion.2
  138.6 0.7 fusion.1
  139.3 1.4 fusion
  (2 shorter events, 0.0 us)
Async XLA Ops:
  6.5 57.2 %copy-start = (f32[8,64,64]{2,1,0:T(8,128)S(1)}, f32[8,64,64]{2,1,0:T(8,128)}, u32[]{:S(2)}) copy-start(f32[8,64,64]{2,1,0:T(8,128)} %param.11) | copy-start | bytes 393220
  6.5 28.6 %copy-start.3 = (s32[32]{0:T(128)S(1)}, s32[32]{0:T(128)}, u32[]{:S(2)}) copy-start(s32[32]{0:T(128)} %param.10) | copy-start | bytes 388
  6.5 57.2 %all-gather.3.cloned.1.call-start = ((), (), s32[]{:S(2)}) async-start(), calls=%async_computation | async-start | bytes 1310720 | tf_op jit(solution)/shard_map/all_gather | solution.py:65
  6.5 8.9 %collective-permute-start = (f32[16,4096]{1,0:T(8,128)}, f32[16,4096]{1,0:T(8,128)S(1)}, u32[]{:S(2)}, u32[]{:S(2)}) collective-permute-start(f32[16,4096]{1,0:T(8,128)} %param.6), channel_id=1, source_target_pairs={{0,4},{4,8},{8,12},{12,16},{16,20},{20,24},{24,28},{28,0},{1,5},{5... | collective-permute-start | bytes 786440 | tf_op jit(solution)/shard_map/ppermute | solution.py:17
  7.0 9.1 %collective-permute-start.1 = (f32[16,4096]{1,0:T(8,128)}, f32[16,4096]{1,0:T(8,128)S(1)}, u32[]{:S(2)}, u32[]{:S(2)}) collective-permute-start(f32[16,4096]{1,0:T(8,128)} %param.6), channel_id=1, source_target_pairs={{4,0},{8,4},{12,8},{16,12},{20,16},{24,20},{28,24},{0,28},{5,1},{9... | collective-permute-start | bytes 786440 | tf_op jit(solution)/shard_map/ppermute | solution.py:19
  34.9 93.3 %all-gather.5.cloned.1.call-start = ((), (), s32[]{:S(2)}) async-start(), calls=%async_computation.1 | async-start | bytes 1310720 | tf_op jit(solution)/shard_map/all_gather | solution.py:65
  63.7 9.6 %copy-start.1 = (f32[64,4096]{1,0:T(8,128)S(1)}, f32[64,4096]{1,0:T(8,128)}, u32[]{:S(2)}) copy-start(f32[64,4096]{1,0:T(8,128)} %all-gather.3.cloned.1.call-done) | copy-start | bytes 3145732
  75.4 8.6 %collective-permute-start.2 = (f32[16,4096]{1,0:T(8,128)S(1)}, f32[16,4096]{1,0:T(8,128)S(1)}, u32[]{:S(2)}, u32[]{:S(2)}) collective-permute-start(f32[16,4096]{1,0:T(8,128)S(1)} %fusion.7), channel_id=1, source_target_pairs={{0,4},{4,8},{8,12},{12,16},{16,20},{20,24},{24,28},{28,0},{1,5},{5... | collective-permute-start | bytes 786440 | tf_op jit(solution)/shard_map/ppermute | solution.py:17
  75.5 8.5 %collective-permute-start.3 = (f32[16,4096]{1,0:T(8,128)S(1)}, f32[16,4096]{1,0:T(8,128)S(1)}, u32[]{:S(2)}, u32[]{:S(2)}) collective-permute-start(f32[16,4096]{1,0:T(8,128)S(1)} %fusion.7), channel_id=1, source_target_pairs={{4,0},{8,4},{12,8},{16,12},{20,16},{24,20},{28,24},{0,28},{5,1},{9... | collective-permute-start | bytes 786440 | tf_op jit(solution)/shard_map/ppermute | solution.py:19
  128.3 9.6 %copy-start.2 = (f32[64,4096]{1,0:T(8,128)S(1)}, f32[64,4096]{1,0:T(8,128)}, u32[]{:S(2)}) copy-start(f32[64,4096]{1,0:T(8,128)} %all-gather.5.cloned.1.call-done) | copy-start | bytes 3145732
Sparse Core Ops, SparseCore 0:
  35.1 28.6 all-gather.2
  102.1 26.1 all-gather.4
where the time goes:
time: 148 us; the launch traced here: 147 us
  waiting for transfers between devices  60.5 us (41%)
  matrix products  56.4 us (38%)
  between operations  13.6 us (9%)
  starting transfers between devices  8.36 us (6%)
  local copies, waits for them, and re-layouts  5.6 us (4%)
  other arithmetic  3.04 us (2%)
    all_gather x2, waiting for transfers between devices, body(): whole = lax.all_gather(moved, 'tracer', axis=0, tiled=True)  54.5 us
    dot_general x2, matrix products, body(): jnp.einsum('sij,qsj->qsi', blocks, picked, precision=lax.Precision.HIGHEST)  30.9 us
    dot_general x16, matrix products, chemistry(): jnp.einsum('ts,tc->sc', jac_table[regime_id], moved, precision=lax.Precis...  23.9 us
    ppermute x2, starting transfers between devices, with_halo(): lax.ppermute(head, axis, [((i + 1) % count, i) for i in range(count)])  7.63 us
    ppermute x2, waiting for transfers between devices, with_halo(): lax.ppermute(tail, axis, [(i, (i + 1) % count) for i in range(count)])  5.33 us
  transfers between devices with their start and end apart: 6, of which 5 were waited for; matrix products, arithmetic and copies ran while one was open for 3% of the time, Pallas kernels for 0%

commit v1 on v0

v1 whole, which is shorter than its diff:
```python
import functools

import jax
import jax.numpy as jnp
from jax import lax
from jax.experimental import pallas as pl
from jax.experimental.pallas import tpu as pltpu
from jax.sharding import PartitionSpec as P

BLOCK = 128
STEPS = 2
KMAX = 4
CHUNKS = 8
UNROLL = 4


def split(v):
    high = v.astype(jnp.bfloat16).astype(jnp.float32)
    return high, v - high


def kernel(n_cells, n_tracer, row_ptr, col_idx, regime, adjoint, blocks, jac, out,
           raw, weights, jt, ext, halves, sent, arrived, back,
           raw_sem, near_sem, first_send, first_recv, to_send, to_recv,
           back_send, back_recv, halo_send, halo_recv, out_sem):
    spec, cells = adjoint.shape
    slots = blocks.shape[0]
    nb = cells // BLOCK
    rows = nb // n_tracer
    part = cells // n_tracer
    nb_total = nb * n_cells
    d = lax.axis_index("cells")
    t = lax.axis_index("tracer")
    right = lax.rem(d + 1, n_cells)
    left = lax.rem(d + n_cells - 1, n_cells)

    per = slots // CHUNKS
    raw_copies = [
        pltpu.make_async_copy(blocks.at[pl.ds(c * per, per)], raw.at[pl.ds(c * per, per)], raw_sem.at[c])
        for c in range(CHUNKS)
    ]

    barrier = pltpu.get_barrier_semaphore()
    pl.semaphore_signal(barrier, inc=1, device_id={"cells": left}, device_id_type=pl.DeviceIdType.MESH)
    pl.semaphore_signal(barrier, inc=1, device_id={"cells": right}, device_id_type=pl.DeviceIdType.MESH)
    for p in range(1, n_tracer):
        pl.semaphore_signal(barrier, inc=1, device_id={"tracer": lax.rem(t + p, n_tracer)},
                            device_id_type=pl.DeviceIdType.MESH)
    near = pltpu.make_async_copy(adjoint, ext.at[0, :, pl.ds(cells, cells)], near_sem)
    near.start()
    for copy in raw_copies:
        copy.start()
    pl.semaphore_wait(barrier, n_tracer + 1)

    def remote(src, dst, send, recv, where):
        return pltpu.make_async_remote_copy(
            src_ref=src, dst_ref=dst, send_sem=send, recv_sem=recv,
            device_id=where, device_id_type=pl.DeviceIdType.MESH)

    first = [
        remote(adjoint, ext.at[0, :, pl.ds(0, cells)], first_send.at[0], first_recv.at[0], {"cells": right}),
        remote(adjoint, ext.at[0, :, pl.ds(2 * cells, cells)], first_send.at[1], first_recv.at[1], {"cells": left}),
    ]
    for copy in first:
        copy.start()

    for r in range(jac.shape[0]):
        high, low = split(jnp.transpose(jac[r]))
        jt[r] = jnp.concatenate([high, low], axis=0).astype(jnp.bfloat16)
    for c in range(CHUNKS):
        raw_copies[c].wait()

        def prepare(s, carry):
            high, low = split(raw[s])
            weights[s, 0:BLOCK] = high.astype(jnp.bfloat16)
            weights[s, BLOCK:2 * BLOCK] = low.astype(jnp.bfloat16)
            return carry

        lax.fori_loop(c * per, (c + 1) * per, prepare, 0, unroll=2)

    def take_in(step, begin, count):
        def one(i, carry):
            g = begin + i
            high, low = split(ext[step, :, pl.ds(pl.multiple_of(g * BLOCK, BLOCK), BLOCK)])
            halves[g] = jnp.concatenate([high, low], axis=0).astype(jnp.bfloat16)
            return carry

        lax.fori_loop(0, count, one, 0, unroll=min(UNROLL, count))

    halves[3 * nb] = jnp.zeros((2 * spec, BLOCK), jnp.bfloat16)
    near.wait()
    take_in(0, nb, nb)
    for copy, third in zip(first, (0, 2)):
        copy.wait_recv()
        take_in(0, third * nb, nb)

    def moved_row(row):
        begin = row_ptr[0, row]
        end = row_ptr[0, row + 1]
        xs, ws = [], []
        for k in range(KMAX):
            live = begin + k < end
            slot = jnp.minimum(begin + k, slots - 1)
            column = col_idx[slot] - (d - 1) * nb
            column = jnp.where(column < 0, column + nb_total, column)
            column = jnp.where(column >= nb_total, column - nb_total, column)
            column = jnp.where(live, jnp.clip(column, 0, 3 * nb - 1), 3 * nb)
            xs.append(halves[column])
            ws.append(weights[slot])
        lhs = jnp.concatenate(xs, axis=1)
        got = lax.dot_general(lhs, jnp.concatenate(ws, axis=1), (((1,), (1,)), ((), ())),
                              preferred_element_type=jnp.float32)
        got = got[:, 0:BLOCK] + got[:, BLOCK:2 * BLOCK]
        return got[0:spec] + got[spec:2 * spec]

    pending = list(first)
    for step in range(STEPS):
        to = []
        for p in list(range(1, n_tracer)) + [0]:
            owner = lax.rem(t + p, n_tracer)

            def transport(i, carry, p=p, owner=owner):
                y = moved_row(owner * rows + i)
                where = pl.ds(pl.multiple_of(i * BLOCK, BLOCK), BLOCK)
                if p:
                    sent[step, p, :, where] = y
                else:
                    arrived[step, t, :, where] = y
                return carry

            lax.fori_loop(0, rows, transport, 0, unroll=min(UNROLL, rows))
            if p:
                copy = remote(sent.at[step, p], arrived.at[step, t], to_send.at[step, p],
                              to_recv.at[step, p], {"tracer": owner})
                copy.start()
                to.append(copy)
        for copy in to:
            copy.wait_recv()
        pending += to

        last = step == STEPS - 1
        for b in range(rows):
            cols = pl.ds(b * BLOCK, BLOCK)
            m = jnp.concatenate([arrived[step, q, :, cols] for q in range(n_tracer)], axis=0)
            high, low = split(m)
            got = lax.dot_general(jt[regime[t * rows + b]],
                                  jnp.concatenate([high, low], axis=1).astype(jnp.bfloat16),
                                  (((1,), (0,)), ((), ())), preferred_element_type=jnp.float32)
            got = got[:, 0:BLOCK] + got[:, BLOCK:2 * BLOCK]
            half = got.shape[0] // 2
            got = got[0:half] + got[half:]
            for q in range(n_tracer):
                back[step, q, :, cols] = got[q * spec:(q + 1) * spec]

        mine = pl.ds(pl.multiple_of(t * part, BLOCK), part)
        centre = pl.ds(pl.multiple_of(cells + t * part, BLOCK), part)
        returned = []
        for p in range(1, n_tracer):
            q = lax.rem(t + p, n_tracer)
            target = out.at[:, mine] if last else ext.at[step + 1, :, centre]
            copy = remote(back.at[step, q], target, back_send.at[step, p], back_recv.at[step, p], {"tracer": q})
            copy.start()
            returned.append(copy)
        pending += returned
        if last:
            own = pltpu.make_async_copy(back.at[step, t], out.at[:, mine], out_sem)
            own.start()
            for copy in returned:
                copy.wait_recv()
            own.wait()
        else:
            ext[step + 1, :, centre] = back[step, t]
            halo = []
            for p in range(n_tracer):
                q = lax.rem(t + n_tracer - p, n_tracer)
                if p:
                    returned[p - 1].wait_recv()

                def place(third, q=q):
                    return ext.at[step + 1, :, pl.ds(pl.multiple_of(third * cells + q * part, BLOCK), part)]

                for side, (third, where) in enumerate(((0, right), (2, left))):
                    copy = remote(place(1), place(third), halo_send.at[step, side, p],
                                  halo_recv.at[step, side, p], {"cells": where})
                    copy.start()
                    halo.append((copy, third * nb + q * rows))
                take_in(step + 1, nb + q * rows, rows)
            for copy, begin in halo:
                copy.wait_recv()
                take_in(step + 1, begin, rows)
            pending += [copy for copy, _ in halo]
    for copy in pending:
        copy.wait_send()


def body(adjoint, blocks, row_ptr, col_idx, regime, jac, n_cells, n_tracer):
    spec, cells = adjoint.shape
    slots = blocks.shape[0]
    part = cells // n_tracer
    f32, bf16 = jnp.float32, jnp.bfloat16
    dma = pltpu.SemaphoreType.DMA
    smem = pl.BlockSpec(memory_space=pltpu.SMEM)
    return pl.pallas_call(
        functools.partial(kernel, n_cells, n_tracer),
        out_shape=jax.ShapeDtypeStruct((spec, cells), f32),
        in_specs=[smem, smem, smem,
                  pl.BlockSpec(memory_space=pl.ANY), pl.BlockSpec(memory_space=pl.ANY),
                  pl.BlockSpec(memory_space=pltpu.VMEM)],
        out_specs=pl.BlockSpec(memory_space=pl.ANY),
        scratch_shapes=[
            pltpu.VMEM((slots, BLOCK, BLOCK), f32),
            pltpu.VMEM((slots, 2 * BLOCK, BLOCK), bf16),
            pltpu.VMEM((jac.shape[0], 2 * jac.shape[2], jac.shape[1]), bf16),
            pltpu.VMEM((STEPS, spec, 3 * cells), f32),
            pltpu.VMEM((3 * cells // BLOCK + 1, 2 * spec, BLOCK), bf16),
            pltpu.VMEM((STEPS, n_tracer, spec, part), f32),
            pltpu.VMEM((STEPS, n_tracer, spec, part), f32),
            pltpu.VMEM((STEPS, n_tracer, spec, part), f32),
            dma((CHUNKS,)), dma(()), dma((2,)), dma((2,)),
            dma((STEPS, n_tracer)), dma((STEPS, n_tracer)),
            dma((STEPS, n_tracer)), dma((STEPS, n_tracer)),
            dma((STEPS, 2, n_tracer)), dma((STEPS, 2, n_tracer)), dma(()),
        ],
        compiler_params=pltpu.CompilerParams(
            collective_id=0, has_side_effects=True, vmem_limit_bytes=40 * 2**20),
    )(row_ptr, col_idx, regime, adjoint, blocks, jac)


def solution(mesh):
    return jax.shard_map(
        functools.partial(body, n_cells=mesh.shape["cells"], n_tracer=mesh.shape["tracer"]),
        mesh=mesh,
        in_specs=(
            P("tracer", "cells"),
            P("cells", None, None),
            P("cells", None),
            P("cells"),
            P("cells"),
            P(),
        ),
        out_specs=P("tracer", "cells"),
        check_vma=False,
    )
```

time: 148 us -> 47 us (0.32)
  waiting for transfers between devices: 60.5 us -> 0 us
  matrix products: 56.4 us -> 0 us
  Pallas kernels: 0 us -> 38.8 us
  between operations: 13.6 us -> 0.02 us
  starting transfers between devices: 8.36 us -> 0 us
  other arithmetic: 3.04 us -> 0 us
  local copies, waits for them, and re-layouts: 5.6 us -> 7.95 us
    dot_general x20 -> x0, matrix products: 56.4 us -> none  [the longest x2 30.9 us: body(): jnp.einsum('sij,qsj->qsi', blocks, picked, precision=lax.Precision.HIGHEST)]
    all_gather x2 -> x0, waiting for transfers between devices: 54.5 us -> none  [body(): whole = lax.all_gather(moved, 'tracer', axis=0, tiled=True)]
    pallas_call x0 -> x1, Pallas kernels: none -> 38.8 us  [body(): pl.pallas_call(functools.partial(kernel, n_cells, n_tracer), out_shape=ja...]
    ppermute x4 -> x0, starting transfers between devices: 8.14 us -> none  [the longest x2 7.63 us: with_halo(): lax.ppermute(head, axis, [((i + 1) % count, i) for i in range(count)])]
    unnamed x10 -> x13, local copies, waits for them, and re-layouts: 1.73 us -> 7.95 us
    ppermute x4 -> x0, waiting for transfers between devices: 5.92 us -> none  [the longest x2 5.33 us: with_halo(): lax.ppermute(tail, axis, [(i, (i + 1) % count) for i in range(count)])]
    gather x2 -> x0, local copies, waits for them, and re-layouts: 1.52 us -> none  [body(): picked = jnp.take(extended_blocks, local_col, axis=1, mode='clip')]
  transfers between devices with their start and end apart: 6 -> 0, of which waited for: 5 -> 0; matrix products, arithmetic and copies ran while one was open for 3% -> 0% of each run, Pallas kernels for 0% -> 0%
where the time goes in v1:
time: 47 us; the launch traced here: 46.8 us
  Pallas kernels  38.8 us (83%)
  local copies, waits for them, and re-layouts  7.95 us (17%)
    pallas_call x1, Pallas kernels, body(): pl.pallas_call(functools.partial(kernel, n_cells, n_tracer), out_shape=ja...  38.8 us
    unnamed x13, local copies, waits for them, and re-layouts  7.95 us

profile of v1, /device:TPU:0, one launch (start us, length us, event | category | flops | bytes accessed | tf_op | source)
XLA Modules:
  0.0 46.8 jit_solution(13509662331962218105)
XLA Ops:
  0.0 0.0 copy-start
  0.0 3.4 %copy-done = f32[128,128,128]{2,1,0:T(8,128)S(1)} copy-done((f32[128,128,128]{2,1,0:T(8,128)S(1)}, f32[128,128,128]{2,1,0:T(8,128)}, u32[]{:S(2)}) %copy-start) | copy-done | bytes 8388632
  3.4 0.0 copy-start.1
  3.4 0.9 %copy-done.1 = f32[16,4096]{1,0:T(8,128)S(1)} copy-done((f32[16,4096]{1,0:T(8,128)S(1)}, f32[16,4096]{1,0:T(8,128)}, u32[]{:S(2)}) %copy-start.1) | copy-done | bytes 262168
  4.3 0.0 copy-start.2
  4.3 0.9 %copy-done.2 = f32[8,64,64]{2,1,0:T(8,128)S(1)} copy-done((f32[8,64,64]{2,1,0:T(8,128)S(1)}, f32[8,64,64]{2,1,0:T(8,128)}, u32[]{:S(2)}) %copy-start.2) | copy-done | bytes 131096
  5.3 0.0 copy-start.3
  5.3 0.7 %copy-done.3 = s32[1,33]{1,0:T(1,128)S(1)} copy-done((s32[1,33]{1,0:T(1,128)S(1)}, s32[1,33]{1,0:T(1,128)}, u32[]{:S(2)}) %copy-start.3) | copy-done | bytes 156
  5.9 0.0 copy-start.4
  5.9 0.7 %copy-done.4 = s32[128]{0:T(128)S(1)} copy-done((s32[128]{0:T(128)S(1)}, s32[128]{0:T(128)}, u32[]{:S(2)}) %copy-start.4) | copy-done | bytes 536
  6.6 0.0 copy-start.5
  6.6 0.7 %copy-done.5 = s32[32]{0:T(128)S(1)} copy-done((s32[32]{0:T(128)S(1)}, s32[32]{0:T(128)}, u32[]{:S(2)}) %copy-start.5) | copy-done | bytes 152
  7.3 38.8 %shard_map.64 = f32[16,4096]{1,0:T(8,128)S(1)} custom-call(s32[1,33]{1,0:T(1,128)S(1)} %copy-done.3, s32[128]{0:T(128)S(1)} %copy-done.4, s32[32]{0:T(128)S(1)} %copy-done.5, f32[16,4096]{1,0:T(8,128)S(1)} %copy-done.1, f32[128,128,128]{2,1,0:T(8,128)S(1)} %copy-done, f32[8,64,64]{2,1,0:T(8,128)S(1)} %copy-done.2), custom_call_target="tpu_custom_call" | custom-call | tf_op jit(solution)/shard_map/pallas_call | solution.py:203
  46.1 0.7 %copy.8 = f32[16,4096]{1,0:T(8,128)} copy(f32[16,4096]{1,0:T(8,128)S(1)} %shard_map.64) | data formatting | bytes 524288
Async XLA Ops:
  0.0 3.4 %copy-start = (f32[128,128,128]{2,1,0:T(8,128)S(1)}, f32[128,128,128]{2,1,0:T(8,128)}, u32[]{:S(2)}) copy-start(f32[128,128,128]{2,1,0:T(8,128)} %blocks.1) | copy-start | bytes 25165828
  3.4 0.9 %copy-start.1 = (f32[16,4096]{1,0:T(8,128)S(1)}, f32[16,4096]{1,0:T(8,128)}, u32[]{:S(2)}) copy-start(f32[16,4096]{1,0:T(8,128)} %adjoint.1) | copy-start | bytes 786436
  4.3 0.9 %copy-start.2 = (f32[8,64,64]{2,1,0:T(8,128)S(1)}, f32[8,64,64]{2,1,0:T(8,128)}, u32[]{:S(2)}) copy-start(f32[8,64,64]{2,1,0:T(8,128)} %jac.1) | copy-start | bytes 393220
  5.3 0.7 %copy-start.3 = (s32[1,33]{1,0:T(1,128)S(1)}, s32[1,33]{1,0:T(1,128)}, u32[]{:S(2)}) copy-start(s32[1,33]{1,0:T(1,128)} %row_ptr.1) | copy-start | bytes 400
  5.9 0.7 %copy-start.4 = (s32[128]{0:T(128)S(1)}, s32[128]{0:T(128)}, u32[]{:S(2)}) copy-start(s32[128]{0:T(128)} %col_idx.1) | copy-start | bytes 1540
  6.6 0.7 %copy-start.5 = (s32[32]{0:T(128)S(1)}, s32[32]{0:T(128)}, u32[]{:S(2)}) copy-start(s32[32]{0:T(128)} %regime.1) | copy-start | bytes 388

commit v2 on v1

--- a/solution.py
+++ b/solution.py
@@ -19,10 +19,10 @@
     return high, v - high
 
 
-def kernel(n_cells, n_tracer, row_ptr, col_idx, regime, adjoint, blocks, jac, out,
-           raw, weights, jt, ext, halves, sent, arrived, back,
+def kernel(n_cells, n_tracer, row_ptr_hbm, col_idx_hbm, regime_hbm, adjoint, blocks, jac_hbm, out,
+           row_ptr, col_idx, regime, jac, raw, weights, jt, ext, halves, sent, arrived, back,
            raw_sem, near_sem, first_send, first_recv, to_send, to_recv,
-           back_send, back_recv, halo_send, halo_recv, out_sem):
+           back_send, back_recv, halo_send, halo_recv, out_sem, small_sem):
     spec, cells = adjoint.shape
     slots = blocks.shape[0]
     nb = cells // BLOCK
@@ -48,6 +48,13 @@
                             device_id_type=pl.DeviceIdType.MESH)
     near = pltpu.make_async_copy(adjoint, ext.at[0, :, pl.ds(cells, cells)], near_sem)
     near.start()
+    small = [
+        pltpu.make_async_copy(source, here, small_sem.at[i])
+        for i, (source, here) in enumerate(
+            ((row_ptr_hbm, row_ptr), (col_idx_hbm, col_idx), (regime_hbm, regime), (jac_hbm, jac)))
+    ]
+    for copy in small:
+        copy.start()
     for copy in raw_copies:
         copy.start()
     pl.semaphore_wait(barrier, n_tracer + 1)
@@ -64,6 +71,8 @@
     for copy in first:
         copy.start()
 
+    for copy in small:
+        copy.wait()
     for r in range(jac.shape[0]):
         high, low = split(jnp.transpose(jac[r]))
         jt[r] = jnp.concatenate([high, low], axis=0).astype(jnp.bfloat16)
@@ -199,15 +208,16 @@
     part = cells // n_tracer
     f32, bf16 = jnp.float32, jnp.bfloat16
     dma = pltpu.SemaphoreType.DMA
-    smem = pl.BlockSpec(memory_space=pltpu.SMEM)
     return pl.pallas_call(
         functools.partial(kernel, n_cells, n_tracer),
         out_shape=jax.ShapeDtypeStruct((spec, cells), f32),
-        in_specs=[smem, smem, smem,
-                  pl.BlockSpec(memory_space=pl.ANY), pl.BlockSpec(memory_space=pl.ANY),
-                  pl.BlockSpec(memory_space=pltpu.VMEM)],
+        in_specs=[pl.BlockSpec(memory_space=pl.ANY)] * 6,
         out_specs=pl.BlockSpec(memory_space=pl.ANY),
         scratch_shapes=[
+            pltpu.SMEM(row_ptr.shape, row_ptr.dtype),
+            pltpu.SMEM(col_idx.shape, col_idx.dtype),
+            pltpu.SMEM(regime.shape, regime.dtype),
+            pltpu.VMEM(jac.shape, f32),
             pltpu.VMEM((slots, BLOCK, BLOCK), f32),
             pltpu.VMEM((slots, 2 * BLOCK, BLOCK), bf16),
             pltpu.VMEM((jac.shape[0], 2 * jac.shape[2], jac.shape[1]), bf16),
@@ -219,10 +229,10 @@
             dma((CHUNKS,)), dma(()), dma((2,)), dma((2,)),
             dma((STEPS, n_tracer)), dma((STEPS, n_tracer)),
             dma((STEPS, n_tracer)), dma((STEPS, n_tracer)),
-            dma((STEPS, 2, n_tracer)), dma((STEPS, 2, n_tracer)), dma(()),
+            dma((STEPS, 2, n_tracer)), dma((STEPS, 2, n_tracer)), dma(()), dma((4,)),
         ],
         compiler_params=pltpu.CompilerParams(
-            collective_id=0, has_side_effects=True, vmem_limit_bytes=40 * 2**20),
+            collective_id=0, has_side_effects=True, vmem_limit_bytes=60 * 2**20),
     )(row_ptr, col_idx, regime, adjoint, blocks, jac)
 
 

time: 47 us -> 40.4 us (0.86)
  local copies, waits for them, and re-layouts: 7.95 us -> 1.67 us
    unnamed x13 -> x1, local copies, waits for them, and re-layouts: 7.95 us -> 1.67 us
where the time goes in v2:
time: 40.4 us; the launch traced here: 40.2 us
  Pallas kernels  38.5 us (95%)
  local copies, waits for them, and re-layouts  1.67 us (4%)
    pallas_call x1, Pallas kernels, body(): pl.pallas_call(functools.partial(kernel, n_cells, n_tracer), out_shape=ja...  38.5 us
    unnamed x1, local copies, waits for them, and re-layouts  1.67 us

profile of v2, /device:TPU:0, one launch (start us, length us, event | category | flops | bytes accessed | tf_op | source)
XLA Modules:
  0.0 40.2 jit_solution(6332370796841107665)
XLA Ops:
  0.0 38.5 %shard_map.64 = f32[16,4096]{1,0:T(8,128)} custom-call(s32[1,33]{1,0:T(1,128)} %row_ptr_hbm.1, s32[128]{0:T(128)} %col_idx_hbm.1, s32[32]{0:T(128)} %regime_hbm.1, f32[16,4096]{1,0:T(8,128)} %adjoint.1, f32[128,128,128]{2,1,0:T(8,128)} %blocks.1, f32[8,64,64]{2,1,0:T(8,128)} %jac_hbm.1), custom_call_target="tpu_custom_call" | custom-call | tf_op jit(solution)/shard_map/pallas_call | solution.py:211
  38.6 1.7 %copy.8 = f32[16,4096]{1,0:T(8,128)} copy(f32[16,4096]{1,0:T(8,128)} %shard_map.64) | data formatting | bytes 524288

commit v3 on v2

v3 whole, which is shorter than its diff:
```python
import functools
import math

import jax
import jax.numpy as jnp
from jax import lax
from jax.experimental import pallas as pl
from jax.experimental.pallas import tpu as pltpu
from jax.sharding import PartitionSpec as P

BLOCK = 128
STEPS = 2
KMAX = 4
CHUNKS = 8
UNROLL = 4
PIECES = 2
HALO = 4


def split(v):
    high = v.astype(jnp.bfloat16).astype(jnp.float32)
    return high, v - high


def kernel(n_cells, n_tracer, row_ptr_hbm, col_idx_hbm, regime_hbm, adjoint, blocks, jac_hbm, out,
           row_ptr, col_idx, regime, jac, raw, weights, jt, ext, halves, sent, arrived, back,
           raw_sem, near_sem, first_send, first_recv, to_send, to_recv,
           back_send, back_recv, halo_send, halo_recv, out_sem, small_sem):
    spec, cells = adjoint.shape
    slots = blocks.shape[0]
    nb = cells // BLOCK
    rows = nb // n_tracer
    part = cells // n_tracer
    nb_total = nb * n_cells
    pieces = arrived.shape[1]
    piece = part // pieces
    piece_rows = rows // pieces
    d = lax.axis_index("cells")
    t = lax.axis_index("tracer")
    right = lax.rem(d + 1, n_cells)
    left = lax.rem(d + n_cells - 1, n_cells)

    per = slots // CHUNKS
    raw_copies = [
        pltpu.make_async_copy(blocks.at[pl.ds(c * per, per)], raw.at[pl.ds(c * per, per)], raw_sem.at[c])
        for c in range(CHUNKS)
    ]

    barrier = pltpu.get_barrier_semaphore()
    pl.semaphore_signal(barrier, inc=1, device_id={"cells": left}, device_id_type=pl.DeviceIdType.MESH)
    pl.semaphore_signal(barrier, inc=1, device_id={"cells": right}, device_id_type=pl.DeviceIdType.MESH)
    for p in range(1, n_tracer):
        pl.semaphore_signal(barrier, inc=1, device_id={"tracer": lax.rem(t + p, n_tracer)},
                            device_id_type=pl.DeviceIdType.MESH)
    near = pltpu.make_async_copy(adjoint, ext.at[0, :, pl.ds(cells, cells)], near_sem)
    near.start()
    small = [
        pltpu.make_async_copy(source, here, small_sem.at[i])
        for i, (source, here) in enumerate(
            ((row_ptr_hbm, row_ptr), (col_idx_hbm, col_idx), (regime_hbm, regime), (jac_hbm, jac)))
    ]
    for copy in small:
        copy.start()
    pl.semaphore_wait(barrier, n_tracer + 1)

    def remote(src, dst, send, recv, where):
        return pltpu.make_async_remote_copy(
            src_ref=src, dst_ref=dst, send_sem=send, recv_sem=recv,
            device_id=where, device_id_type=pl.DeviceIdType.MESH)

    near.wait()
    wide = cells // HALO
    first = [
        remote(ext.at[0, :, pl.ds(cells + g * wide, wide)], ext.at[0, :, pl.ds(third * cells + g * wide, wide)],
               first_send.at[side, g], first_recv.at[side, g], {"cells": where})
        for g in range(HALO) for side, (third, where) in enumerate(((0, right), (2, left)))
    ]
    for copy in first:
        copy.start()
    for copy in raw_copies:
        copy.start()

    for copy in small:
        copy.wait()
    for r in range(jac.shape[0]):
        high, low = split(jnp.transpose(jac[r]))
        jt[r] = jnp.concatenate([high, low], axis=0).astype(jnp.bfloat16)
    for c in range(CHUNKS):
        raw_copies[c].wait()

        def prepare(s, carry):
            high, low = split(raw[s])
            weights[s, 0:BLOCK] = high.astype(jnp.bfloat16)
            weights[s, BLOCK:2 * BLOCK] = low.astype(jnp.bfloat16)
            return carry

        lax.fori_loop(c * per, (c + 1) * per, prepare, 0, unroll=2)

    def take_in(step, begin, count):
        def one(i, carry):
            g = begin + i
            high, low = split(ext[step, :, pl.ds(pl.multiple_of(g * BLOCK, BLOCK), BLOCK)])
            halves[g] = jnp.concatenate([high, low], axis=0).astype(jnp.bfloat16)
            return carry

        lax.fori_loop(0, count, one, 0, unroll=min(UNROLL, count))

    halves[3 * nb] = jnp.zeros((2 * spec, BLOCK), jnp.bfloat16)
    take_in(0, nb, nb)
    for i, copy in enumerate(first):
        copy.wait_recv()
        take_in(0, (i % 2) * 2 * nb + (i // 2) * (nb // HALO), nb // HALO)

    def moved_row(row):
        begin = row_ptr[0, row]
        end = row_ptr[0, row + 1]
        xs, ws = [], []
        for k in range(KMAX):
            live = begin + k < end
            slot = jnp.minimum(begin + k, slots - 1)
            column = col_idx[slot] - (d - 1) * nb
            column = jnp.where(column < 0, column + nb_total, column)
            column = jnp.where(column >= nb_total, column - nb_total, column)
            column = jnp.where(live, jnp.clip(column, 0, 3 * nb - 1), 3 * nb)
            xs.append(halves[column])
            ws.append(weights[slot])
        lhs = jnp.concatenate(xs, axis=1)
        got = lax.dot_general(lhs, jnp.concatenate(ws, axis=1), (((1,), (1,)), ((), ())),
                              preferred_element_type=jnp.float32)
        got = got[:, 0:BLOCK] + got[:, BLOCK:2 * BLOCK]
        return got[0:spec] + got[spec:2 * spec]

    pending = list(first)
    peers = range(1, n_tracer)
    for step in range(STEPS):
        to = {}
        for h in range(pieces):
            for p in (*peers, 0):
                owner = lax.rem(t + p, n_tracer)

                def transport(i, carry, p=p, h=h, owner=owner):
                    y = moved_row(owner * rows + h * piece_rows + i)
                    where = pl.ds(pl.multiple_of(i * BLOCK, BLOCK), BLOCK)
                    if p:
                        sent[step, h, p, :, where] = y
                    else:
                        arrived[step, h, t, :, where] = y
                    return carry

                lax.fori_loop(0, piece_rows, transport, 0, unroll=min(UNROLL, piece_rows))
                if p:
                    to[h, p] = remote(sent.at[step, h, p], arrived.at[step, h, t], to_send.at[step, h, p],
                                      to_recv.at[step, h, p], {"tracer": owner})
                    to[h, p].start()

        last = step == STEPS - 1
        returned, halo = {}, []

        def place(third, q, h):
            start = third * cells + q * part + h * piece
            return ext.at[step + 1, :, pl.ds(pl.multiple_of(start, BLOCK), piece)]

        def forward(p, h):
            q = lax.rem(t + n_tracer - p, n_tracer)
            for side, (third, where) in enumerate(((0, right), (2, left))):
                copy = remote(place(1, q, h), place(third, q, h), halo_send.at[step, side, h, p],
                              halo_recv.at[step, side, h, p], {"cells": where})
                copy.start()
                halo.append((copy, third * nb + q * rows + h * piece_rows))

        for h in range(pieces):
            for p in peers:
                to[h, p].wait_recv()
            for b in range(piece_rows):
                cols = pl.ds(b * BLOCK, BLOCK)
                m = jnp.concatenate([arrived[step, h, q, :, cols] for q in range(n_tracer)], axis=0)
                high, low = split(m)
                got = lax.dot_general(jt[regime[t * rows + h * piece_rows + b]],
                                      jnp.concatenate([high, low], axis=1).astype(jnp.bfloat16),
                                      (((1,), (0,)), ((), ())), preferred_element_type=jnp.float32)
                got = got[:, 0:BLOCK] + got[:, BLOCK:2 * BLOCK]
                half = got.shape[0] // 2
                got = got[0:half] + got[half:]
                for q in range(n_tracer):
                    back[step, h, q, :, cols] = got[q * spec:(q + 1) * spec]

            mine = pl.ds(pl.multiple_of(t * part + h * piece, BLOCK), piece)
            for p in peers:
                q = lax.rem(t + p, n_tracer)
                target = out.at[:, mine] if last else place(1, t, h)
                returned[h, p] = remote(back.at[step, h, q], target, back_send.at[step, h, p],
                                        back_recv.at[step, h, p], {"tracer": q})
                returned[h, p].start()
            if last:
                pltpu.make_async_copy(back.at[step, h, t], out.at[:, mine], out_sem.at[h]).start()
            else:
                ext[step + 1, :, pl.ds(pl.multiple_of(cells + t * part + h * piece, BLOCK), piece)] = back[step, h, t]
                forward(0, h)
                take_in(step + 1, nb + t * rows + h * piece_rows, piece_rows)
        for h in range(pieces):
            for p in peers:
                returned[h, p].wait_recv()
                if not last:
                    forward(p, h)
                    q = lax.rem(t + n_tracer - p, n_tracer)
                    take_in(step + 1, nb + q * rows + h * piece_rows, piece_rows)
            if last:
                mine = pl.ds(pl.multiple_of(t * part + h * piece, BLOCK), piece)
                pltpu.make_async_copy(back.at[step, h, t], out.at[:, mine], out_sem.at[h]).wait()
        for copy, begin in halo:
            copy.wait_recv()
            take_in(step + 1, begin, piece_rows)
        pending += [*to.values(), *returned.values(), *(copy for copy, _ in halo)]
    for copy in pending:
        copy.wait_send()


def body(adjoint, blocks, row_ptr, col_idx, regime, jac, n_cells, n_tracer):
    spec, cells = adjoint.shape
    slots = blocks.shape[0]
    part = cells // n_tracer
    pieces = math.gcd(PIECES, part // BLOCK)
    f32, bf16 = jnp.float32, jnp.bfloat16
    dma = pltpu.SemaphoreType.DMA
    return pl.pallas_call(
        functools.partial(kernel, n_cells, n_tracer),
        out_shape=jax.ShapeDtypeStruct((spec, cells), f32),
        in_specs=[pl.BlockSpec(memory_space=pl.ANY)] * 6,
        out_specs=pl.BlockSpec(memory_space=pl.ANY),
        scratch_shapes=[
            pltpu.SMEM(row_ptr.shape, row_ptr.dtype),
            pltpu.SMEM(col_idx.shape, col_idx.dtype),
            pltpu.SMEM(regime.shape, regime.dtype),
            pltpu.VMEM(jac.shape, f32),
            pltpu.VMEM((slots, BLOCK, BLOCK), f32),
            pltpu.VMEM((slots, 2 * BLOCK, BLOCK), bf16),
            pltpu.VMEM((jac.shape[0], 2 * jac.shape[2], jac.shape[1]), bf16),
            pltpu.VMEM((STEPS, spec, 3 * cells), f32),
            pltpu.VMEM((3 * cells // BLOCK + 1, 2 * spec, BLOCK), bf16),
            pltpu.VMEM((STEPS, pieces, n_tracer, spec, part // pieces), f32),
            pltpu.VMEM((STEPS, pieces, n_tracer, spec, part // pieces), f32),
            pltpu.VMEM((STEPS, pieces, n_tracer, spec, part // pieces), f32),
            dma((CHUNKS,)), dma(()), dma((2, HALO)), dma((2, HALO)),
            dma((STEPS, pieces, n_tracer)), dma((STEPS, pieces, n_tracer)),
            dma((STEPS, pieces, n_tracer)), dma((STEPS, pieces, n_tracer)),
            dma((STEPS, 2, pieces, n_tracer)), dma((STEPS, 2, pieces, n_tracer)), dma((pieces,)), dma((4,)),
        ],
        compiler_params=pltpu.CompilerParams(
            collective_id=0, has_side_effects=True, vmem_limit_bytes=60 * 2**20),
    )(row_ptr, col_idx, regime, adjoint, blocks, jac)


def solution(mesh):
    return jax.shard_map(
        functools.partial(body, n_cells=mesh.shape["cells"], n_tracer=mesh.shape["tracer"]),
        mesh=mesh,
        in_specs=(
            P("tracer", "cells"),
            P("cells", None, None),
            P("cells", None),
            P("cells"),
            P("cells"),
            P(),
        ),
        out_specs=P("tracer", "cells"),
        check_vma=False,
    )
```

time: 40.4 us -> 38.5 us (0.953)
  Pallas kernels: 38.5 us -> 36.7 us
    pallas_call x1, Pallas kernels: 38.5 us -> 36.7 us  [body(): pl.pallas_call(functools.partial(kernel, n_cells, n_tracer), out_shape=ja...]
where the time goes in v3:
time: 38.5 us; the launch traced here: 38.4 us
  Pallas kernels  36.7 us (95%)
  local copies, waits for them, and re-layouts  1.67 us (4%)
    pallas_call x1, Pallas kernels, body(): pl.pallas_call(functools.partial(kernel, n_cells, n_tracer), out_shape=ja...  36.7 us
    unnamed x1, local copies, waits for them, and re-layouts  1.67 us

profile of v3, /device:TPU:0, one launch (start us, length us, event | category | flops | bytes accessed | tf_op | source)
XLA Modules:
  0.0 38.4 jit_solution(3885519907317633923)
XLA Ops:
  0.0 36.7 %shard_map.64 = f32[16,4096]{1,0:T(8,128)} custom-call(s32[1,33]{1,0:T(1,128)} %row_ptr_hbm.1, s32[128]{0:T(128)} %col_idx_hbm.1, s32[32]{0:T(128)} %regime_hbm.1, f32[16,4096]{1,0:T(8,128)} %adjoint.1, f32[128,128,128]{2,1,0:T(8,128)} %blocks.1, f32[8,64,64]{2,1,0:T(8,128)} %jac_hbm.1), custom_call_target="tpu_custom_call" | custom-call | tf_op jit(solution)/shard_map/pallas_call | solution.py:225
  36.7 1.7 %copy.8 = f32[16,4096]{1,0:T(8,128)} copy(f32[16,4096]{1,0:T(8,128)} %shard_map.64) | data formatting | bytes 524288

commit v4 on v3

--- a/solution.py
+++ b/solution.py
@@ -196,17 +196,16 @@
             else:
                 ext[step + 1, :, pl.ds(pl.multiple_of(cells + t * part + h * piece, BLOCK), piece)] = back[step, h, t]
                 forward(0, h)
-                take_in(step + 1, nb + t * rows + h * piece_rows, piece_rows)
         for h in range(pieces):
             for p in peers:
                 returned[h, p].wait_recv()
                 if not last:
                     forward(p, h)
-                    q = lax.rem(t + n_tracer - p, n_tracer)
-                    take_in(step + 1, nb + q * rows + h * piece_rows, piece_rows)
             if last:
                 mine = pl.ds(pl.multiple_of(t * part + h * piece, BLOCK), piece)
                 pltpu.make_async_copy(back.at[step, h, t], out.at[:, mine], out_sem.at[h]).wait()
+        if not last:
+            take_in(step + 1, nb, nb)
         for copy, begin in halo:
             copy.wait_recv()
             take_in(step + 1, begin, piece_rows)

time: 38.5 us -> 38.5 us (level)
  no operation moved by 1% of the time
where the time goes in v4:
time: 38.5 us; the launch traced here: 38.4 us
  Pallas kernels  36.7 us (95%)
  local copies, waits for them, and re-layouts  1.67 us (4%)
    pallas_call x1, Pallas kernels, body(): pl.pallas_call(functools.partial(kernel, n_cells, n_tracer), out_shape=ja...  36.7 us
    unnamed x1, local copies, waits for them, and re-layouts  1.67 us

profile of v4, /device:TPU:0, one launch (start us, length us, event | category | flops | bytes accessed | tf_op | source)
XLA Modules:
  0.0 38.4 jit_solution(3471142766582550043)
XLA Ops:
  0.0 36.7 %shard_map.64 = f32[16,4096]{1,0:T(8,128)} custom-call(s32[1,33]{1,0:T(1,128)} %row_ptr_hbm.1, s32[128]{0:T(128)} %col_idx_hbm.1, s32[32]{0:T(128)} %regime_hbm.1, f32[16,4096]{1,0:T(8,128)} %adjoint.1, f32[128,128,128]{2,1,0:T(8,128)} %blocks.1, f32[8,64,64]{2,1,0:T(8,128)} %jac_hbm.1), custom_call_target="tpu_custom_call" | custom-call | tf_op jit(solution)/shard_map/pallas_call | solution.py:224
  36.7 1.7 %copy.8 = f32[16,4096]{1,0:T(8,128)} copy(f32[16,4096]{1,0:T(8,128)} %shard_map.64) | data formatting | bytes 524288
